TPU v7x, 512 devices: a whole 4x4x16 slice. The times are simulated.
512 devices in a mesh: dp: 2 (over core), fsdp: 32 (over y, z_lo), tensor: 8 (over z_hi, x).
Axes of the slice: x: 4, y: 4, z: 16 (z_hi: 2, z_lo: 8; z = z_hi * 8 + z_lo), core: 2. Of those that a mesh axis runs over, the one named last changes fastest.
Arguments:
- tokens: bfloat16 [16384, 4096], P(('dp', 'fsdp', 'tensor')), may hold values from -40 to 40
- norm_gain: float32 [4096], replicated, may hold values from 0.5 to 1.5
- tile_values: bfloat16 [512, 128, 128], P(('fsdp', 'tensor')), may hold values from -0.25 to 0.25
- tile_rows: int32 [8, 64], P('tensor'), may hold values from 0 to 31, as said below
- tile_cols: int32 [8, 64], P('tensor'), may hold values from 0 to 13
- tile_counts: int32 [8, 32], P('tensor'), may hold values from 0 to 2, as said below
- grad_out: bfloat16 [16384, 14336], P(('dp', 'fsdp'), 'tensor'), may hold values from -3 to 3
Outputs:
- mixed: bfloat16 [16384, 14336], P(('dp', 'fsdp'), 'tensor')
- grad_x: bfloat16 [16384, 4096], P(('dp', 'fsdp', 'tensor'))
- grad_gain: float32 [4096], replicated
- grad_tiles: float32 [512, 128, 128], P(('fsdp', 'tensor'))
Inputs may be any that keep to these rules, and one draw needn't show every extreme that they name: `tile_counts`: for each tensor index the counts over the 32 fsdp shards sum to 56, and some shard holds exactly 2. `tile_rows`: within one tensor index the (row, column) pairs of held slots are all different.
All inputs are finite; a program needn't handle non-finite values.
Results may differ from a plain program's by a relative error of at most 0.013.
Values may be sent and summed in bfloat16 or wider, within the bound.
A program may use at most 128 MiB of HBM per device.

v0:
```python
import jax
import jax.numpy as jnp
from jax import lax
from jax.sharding import PartitionSpec as P


def tile_forward(group_rows, values, rows_list, cols_list, col_tiles):
    tile_size = values.shape[1]
    blocks = group_rows.reshape(group_rows.shape[0], -1, tile_size)
    picked = jnp.take(blocks, rows_list, axis=1)
    product = jnp.einsum("tsk,skn->tsn", picked, values, preferred_element_type=jnp.float32)
    placed = (
        jnp.zeros((group_rows.shape[0], col_tiles, tile_size), jnp.float32)
        .at[:, cols_list]
        .add(product)
    )
    return placed.reshape(group_rows.shape[0], col_tiles * tile_size)


def tile_backward(grad_rows, values, rows_list, cols_list, row_tiles):
    tile_size = values.shape[1]
    blocks = grad_rows.reshape(grad_rows.shape[0], -1, tile_size)
    picked = jnp.take(blocks, cols_list, axis=1)
    product = jnp.einsum("tsn,skn->tsk", picked, values, preferred_element_type=jnp.float32)
    placed = (
        jnp.zeros((grad_rows.shape[0], row_tiles, tile_size), jnp.float32)
        .at[:, rows_list]
        .add(product)
    )
    return placed.reshape(grad_rows.shape[0], row_tiles * tile_size)


def per_device(tokens, norm_gain, tile_values, tile_rows, tile_cols, tile_counts, grad_out):
    tile_size = tile_values.shape[1]
    slot_cap = tile_values.shape[0]
    row_tiles = tokens.shape[1] // tile_size
    col_tiles = grad_out.shape[1] // tile_size
    rows_list = tile_rows[0]
    cols_list = tile_cols[0]
    shard_counts = tile_counts[0]
    held_all = (jnp.arange(slot_cap)[None, :] < shard_counts[:, None]).reshape(-1)
    own_held = jnp.arange(slot_cap) < shard_counts[lax.axis_index("fsdp")]
    local_float = tokens.astype(jnp.float32)
    inv_rms = lax.rsqrt(jnp.mean(local_float * local_float, axis=1, keepdims=True) + 1e-05)
    scaled = local_float * inv_rms
    normed = (scaled * norm_gain).astype(jnp.bfloat16)
    group_rows = lax.all_gather(normed, "tensor", axis=0, tiled=True)
    gathered = lax.all_gather(tile_values, "fsdp", axis=0, tiled=True)
    kept_values = jnp.where(held_all[:, None, None], gathered, jnp.zeros_like(gathered))
    outputs = tile_forward(group_rows, kept_values, rows_list, cols_list, col_tiles)
    mixed = outputs.astype(jnp.bfloat16)
    input_grad = lax.psum_scatter(
        tile_backward(grad_out, kept_values, rows_list, cols_list, row_tiles).astype(jnp.bfloat16),
        "tensor",
        scatter_dimension=0,
        tiled=True,
    ).astype(jnp.float32)
    x_blocks = group_rows.reshape(group_rows.shape[0], row_tiles, tile_size)
    g_blocks = grad_out.reshape(grad_out.shape[0], col_tiles, tile_size)
    picked_x = jnp.take(x_blocks, rows_list, axis=1)
    picked_g = jnp.take(g_blocks, cols_list, axis=1)
    grad_shard = lax.psum_scatter(
        jnp.einsum("tsk,tsn->skn", picked_x, picked_g, preferred_element_type=jnp.float32),
        "fsdp",
        scatter_dimension=0,
        tiled=True,
    )
    grad_shard = jnp.where(own_held[:, None, None], grad_shard, jnp.zeros_like(grad_shard))
    grad_tiles = lax.psum(grad_shard, "dp")
    gain_part = jnp.sum(input_grad * scaled, axis=0)
    grad_gain = lax.psum(gain_part, ("dp", "fsdp", "tensor"))
    hidden_grad = input_grad * norm_gain
    grad_x = (
        inv_rms * (hidden_grad - scaled * jnp.mean(hidden_grad * scaled, axis=1, keepdims=True))
    ).astype(jnp.bfloat16)
    return (mixed, grad_x, grad_gain, grad_tiles)


def solution(mesh):
    placed = (
        P(("dp", "fsdp", "tensor"), None),
        P(),
        P(("fsdp", "tensor"), None, None),
        P("tensor", None),
        P("tensor", None),
        P("tensor", None),
        P(("dp", "fsdp"), "tensor"),
    )
    return jax.shard_map(
        per_device,
        mesh=mesh,
        in_specs=placed,
        out_specs=(
            P(("dp", "fsdp"), "tensor"),
            P(("dp", "fsdp", "tensor"), None),
            P(),
            P(("fsdp", "tensor"), None, None),
        ),
        check_vma=False,
    )
```

profile of v0, /device:TPU:1, one launch (start us, length us, event | category | flops | bytes accessed | tf_op | source)
XLA Modules:
  0.0 848.5 jit_solution(9026113694259479338)
XLA Ops:
  7.2 0.0 all-gather.3.cloned.1.call-start
  7.2 0.7 all-gather.3.cloned.1.call-update
  7.9 0.0 reduce-scatter.7.cloned.1.call-start
  7.9 1.5 copy.32
  9.4 0.6 copy.33
  10.0 0.7 iota_compare_fusion
  10.8 0.1 lt.72
  10.9 0.7 compare_select_fusion
  11.6 0.0 copy-start.5
  11.6 3.1 gather_fusion.1
  14.6 0.0 copy-done.4
  14.7 207.7 %all-gather.3.cloned.1.call-done = bf16[64,128,128]{2,1,0:T(8,128)(2,1)} async-done(((bf16[2,128,128]{2,1,0:T(8,128)(2,1)}), bf16[64,128,128]{2,1,0:T(8,128)(2,1)}) %all-gather.3.cloned.1.call-update) | async-done | bytes 2097168 | tf_op jit(solution)/shard_map/all_gather | solution.py:48
  222.3 7.4 fusion.2
  229.8 2.4 broadcast_in_dim.57
  232.2 19.4 %scatter_fusion.1 = f32[256,32,128]{2,0,1:T(8,128)} fusion(f32[256,32,128]{2,0,1:T(8,128)} %broadcast_in_dim.57, s32[64]{0:T(128)S(1)} %fusion.18, f32[64,256,128]{2,1,0:T(8,128)} %fusion.2), kind=kCustom, calls=%fused_computation.3 | custom fusion | flops 2097152 | bytes 25166080 | tf_op jit(solution)/shard_map/scatter-add | solution.py:28
  251.6 2.5 convert_element_type.28
  254.1 2.9 copy.34
  257.0 4.1 copy.39
  261.2 0.0 reduce-scatter.7.cloned.1.call-update
  261.2 0.0 all-gather.5.cloned.1.call-start
  261.2 0.2 fusion.15
  261.4 162.8 %reduce-scatter.7.cloned.1.call-done = bf16[32,4096]{1,0:T(8,128)(2,1)} async-done(((bf16[256,4096]{1,0:T(8,128)(2,1)}), bf16[32,4096]{1,0:T(8,128)(2,1)}) %reduce-scatter.7.cloned.1.call-update) | async-done | bytes 262160 | tf_op jit(solution)/shard_map/reduce_scatter | solution.py:52
  424.3 1.3 fusion.16
  425.5 1.9 fusion.12
  427.5 0.0 all-gather.5.cloned.1.call-update
  427.5 0.0 reduce-scatter.5.cloned.1.call-start
  427.6 109.9 %all-gather.5.cloned.1.call-done = bf16[256,4096]{1,0:T(8,128)(2,1)} async-done(((bf16[32,4096]{1,0:T(8,128)(2,1)}), bf16[256,4096]{1,0:T(8,128)(2,1)}) %all-gather.5.cloned.1.call-update) | async-done | bytes 2097168 | tf_op jit(solution)/shard_map/all_gather | solution.py:47
  537.5 4.1 copy.29
  541.6 3.2 copy.30
  544.8 3.0 gather_fusion
  547.8 7.0 fusion
  554.8 0.0 reduce-scatter.5.cloned.1.call-update
  554.9 0.0 all-reduce.2.cloned.1.call-start
  554.9 0.6 copy-done.3
  555.5 0.6 constant_dynamic-slice_fusion
  556.1 0.6 iota_compare_fusion.1
  556.7 103.2 %psum.14 = f32[4096]{0:T(1024)} all-reduce(f32[4096]{0:T(1024)S(1)} %get-tuple-element.18), channel_id=1, replica_groups=mesh['dp'=2,'fsdp'=32,'tensor'=8] {'dp','fsdp','tensor'}, use_global_device_ids=true, to_apply=%region_6.9 | all-reduce | flops 4096 | bytes 32768 | tf_op jit(solution)/shard_map/psum | solution.py:71
  659.9 119.5 %reduce-scatter.5.cloned.1.call-done = f32[2,128,128]{2,1,0:T(8,128)} async-done(((f32[64,128,128]{2,1,0:T(8,128)}), f32[2,128,128]{2,1,0:T(8,128)}) %reduce-scatter.5.cloned.1.call-update) | async-done | bytes 131088 | tf_op jit(solution)/shard_map/reduce_scatter | solution.py:62
  779.5 1.6 broadcast_select_fusion.9
  781.1 0.0 all-reduce.2.cloned.1.call-update
  781.1 6.7 fusion.5
  787.9 0.2 broadcast_in_dim.54
  788.0 12.4 %scatter_fusion = f32[256,14,128]{2,0,1:T(8,128)S(1)} fusion(f32[256,14,128]{2,0,1:T(8,128)S(1)} %broadcast_in_dim.54, s32[64]{0:T(128)S(1)} %fusion.17, f32[64,256,128]{2,1,0:T(8,128)} %fusion.5), kind=kCustom, calls=%fused_computation.2 | custom fusion | flops 2097152 | bytes 25166080 | tf_op jit(solution)/shard_map/scatter-add | solution.py:15
  800.5 0.2 convert_element_type.26
  800.6 0.5 copy.31
  801.2 1.4 copy.37
  802.5 37.8 %all-reduce.2.cloned.1.call-done = f32[2,128,128]{2,1,0:T(8,128)} async-done(((f32[2,128,128]{2,1,0:T(8,128)}), f32[2,128,128]{2,1,0:T(8,128)}) %all-reduce.2.cloned.1.call-update) | async-done | bytes 131088 | tf_op jit(solution)/shard_map/psum | solution.py:69
  840.4 1.6 copy.44
  (17 shorter events, 0.1 us)
Async XLA Ops:
  7.2 215.2 %all-gather.3.cloned.1.call-start = ((), (), s32[]{:S(2)}) async-start(), calls=%async_computation.2 | async-start | bytes 2162688 | tf_op jit(solution)/shard_map/all_gather | solution.py:48
  7.9 416.4 %reduce-scatter.7.cloned.1.call-start = ((), (), s32[]{:S(2)}) async-start(), calls=%async_computation.6 | async-start | bytes 2359296 | tf_op jit(solution)/shard_map/reduce_scatter | solution.py:52
  11.6 3.1 copy-start.4
  11.6 3.1 copy-start.5
  257.0 4.2 copy-start.1
  257.0 167.2 %copy-start.2 = (f32[4096]{0:T(1024)S(1)}, f32[4096]{0:T(1024)}, u32[]{:S(2)}) copy-start(f32[4096]{0:T(1024)} %param.12) | copy-start | bytes 49156
  261.2 276.3 %all-gather.5.cloned.1.call-start = ((), (), s32[]{:S(2)}) async-start(), calls=%async_computation.3 | async-start | bytes 2359296 | tf_op jit(solution)/shard_map/all_gather | solution.py:47
  427.5 352.0 %reduce-scatter.5.cloned.1.call-start = ((), (), s32[]{:S(2)}) async-start(), calls=%async_computation.4 | async-start | bytes 4325376 | tf_op jit(solution)/shard_map/reduce_scatter | solution.py:62
  554.8 0.7 copy-start.3
  554.8 226.3 %copy-start = (bf16[64,128,128]{2,1,0:T(8,128)(2,1)S(1)}, bf16[64,128,128]{2,1,0:T(8,128)(2,1)}, u32[]{:S(2)}) copy-start(bf16[64,128,128]{2,1,0:T(8,128)(2,1)} %all-gather.3.cloned.1.call-done) | copy-start | bytes 6291460
  554.9 285.5 %all-reduce.2.cloned.1.call-start = ((), (), s32[]{:S(2)}) async-start(), calls=%async_computation.5 | async-start | bytes 262144 | tf_op jit(solution)/shard_map/psum | solution.py:69
Sparse Core Ops, SparseCore 0:
  10.1 212.2 all-gather.2
  261.3 162.8 reduce-scatter.6
  428.5 108.9 all-gather.4
  555.0 224.4 reduce-scatter.4
  783.0 57.3 all-reduce.1
where the time goes:
time: 849 us; the launch traced here: 848 us
  waiting for transfers between devices  639 us (75%)
  blocking collectives  103 us (12%)
  other arithmetic  41.6 us (5%)
  local copies, waits for them, and re-layouts  29.9 us (4%)
  matrix products  21.2 us (2%)
  between operations  13.9 us (2%)
    all_gather x1, waiting for transfers between devices, per_device(): gathered = lax.all_gather(tile_values, 'fsdp', axis=0, tiled=True)  208 us
    reduce_scatter x1, waiting for transfers between devices, per_device(): lax.psum_scatter(tile_backward(grad_out, kept_values, rows_list, cols_lis...  163 us
    reduce_scatter x1, waiting for transfers between devices, per_device(): lax.psum_scatter(jnp.einsum('tsk,tsn->skn', picked_x, picked_g, preferred...  120 us
    all_gather x1, waiting for transfers between devices, per_device(): group_rows = lax.all_gather(normed, 'tensor', axis=0, tiled=True)  110 us
    psum x1, blocking collectives, per_device(): grad_gain = lax.psum(gain_part, ('dp', 'fsdp', 'tensor'))  103 us
    psum x1, waiting for transfers between devices, per_device(): grad_tiles = lax.psum(grad_shard, 'dp')  37.8 us
    scatter-add x1, other arithmetic, tile_backward(): placed = jnp.zeros((grad_rows.shape[0], row_tiles, tile_size), jnp.float3...  19.4 us
  transfers between devices with their start and end apart: 5, of which 5 were waited for; matrix products, arithmetic and copies ran while one was open for 3% of the time, Pallas kernels for 0%

commit v1 on v0

--- a/solution.py
+++ b/solution.py
@@ -45,7 +45,10 @@
     scaled = local_float * inv_rms
     normed = (scaled * norm_gain).astype(jnp.bfloat16)
     group_rows = lax.all_gather(normed, "tensor", axis=0, tiled=True)
-    gathered = lax.all_gather(tile_values, "fsdp", axis=0, tiled=True)
+    size = lax.axis_size("fsdp")
+    parts = jnp.stack([tile_values for _ in range(size)])
+    parts = lax.all_to_all(parts, "fsdp", split_axis=0, concat_axis=0)
+    gathered = jnp.concatenate(parts, axis=0)
     kept_values = jnp.where(held_all[:, None, None], gathered, jnp.zeros_like(gathered))
     outputs = tile_forward(group_rows, kept_values, rows_list, cols_list, col_tiles)
     mixed = outputs.astype(jnp.bfloat16)

time: 849 us -> 727 us (0.86)
  waiting for transfers between devices: 639 us -> 498 us
  starting transfers between devices: 0.2 us -> 16.4 us
    all_gather x1 -> x0, waiting for transfers between devices: 208 us -> none  [per_device(): gathered = lax.all_gather(tile_values, 'fsdp', axis=0, tiled=True)]
    all_to_all x0 -> x1, waiting for transfers between devices: none -> 86.3 us  [per_device(): parts = lax.all_to_all(parts, 'fsdp', split_axis=0, concat_axis=0)]
    reduce_scatter x1, waiting for transfers between devices: 163 us -> 145 us  [per_device(): lax.psum_scatter(tile_backward(grad_out, kept_values, rows_list, cols_lis...]
    all_to_all x0 -> x1, starting transfers between devices: none -> 16.2 us  [per_device(): parts = lax.all_to_all(parts, 'fsdp', split_axis=0, concat_axis=0)]
  transfers between devices with their start and end apart: 5 -> 5, of which waited for: 5 -> 5; matrix products, arithmetic and copies ran while one was open for 3% -> 4% of each run, Pallas kernels for 0% -> 0%
where the time goes in v1:
time: 727 us; the launch traced here: 726 us
  waiting for transfers between devices  498 us (69%)
  blocking collectives  103 us (14%)
  other arithmetic  40.6 us (6%)
  local copies, waits for them, and re-layouts  35.4 us (5%)
  matrix products  18.2 us (3%)
  starting transfers between devices  16.4 us (2%)
  between operations  14 us (2%)
    reduce_scatter x1, waiting for transfers between devices, per_device(): lax.psum_scatter(tile_backward(grad_out, kept_values, rows_list, cols_lis...  145 us
    reduce_scatter x1, waiting for transfers between devices, per_device(): lax.psum_scatter(jnp.einsum('tsk,tsn->skn', picked_x, picked_g, preferred...  121 us
    all_gather x1, waiting for transfers between devices, per_device(): group_rows = lax.all_gather(normed, 'tensor', axis=0, tiled=True)  110 us
    psum x1, blocking collectives, per_device(): grad_gain = lax.psum(gain_part, ('dp', 'fsdp', 'tensor'))  103 us
    all_to_all x1, waiting for transfers between devices, per_device(): parts = lax.all_to_all(parts, 'fsdp', split_axis=0, concat_axis=0)  86.3 us
    psum x1, waiting for transfers between devices, per_device(): grad_tiles = lax.psum(grad_shard, 'dp')  36.2 us
    scatter-add x1, other arithmetic, tile_backward(): placed = jnp.zeros((grad_rows.shape[0], row_tiles, tile_size), jnp.float3...  19.4 us
    all_to_all x1, starting transfers between devices, per_device(): parts = lax.all_to_all(parts, 'fsdp', split_axis=0, concat_axis=0)  16.2 us
  transfers between devices with their start and end apart: 5, of which 5 were waited for; matrix products, arithmetic and copies ran while one was open for 4% of the time, Pallas kernels for 0%

profile of v1, /device:TPU:1, one launch (start us, length us, event | category | flops | bytes accessed | tf_op | source)
XLA Modules:
  0.0 726.1 jit_solution(1442723272345168450)
XLA Ops:
  7.2 0.0 copy-start.4
  7.2 2.8 stack.2
  10.0 16.2 %all-to-all-start = ((bf16[32,2,128,128]{3,2,1,0:T(8,128)(2,1)}), bf16[32,2,128,128]{3,2,1,0:T(8,128)(2,1)S(1)}, u32[]{:S(2)}, u32[]{:S(2)}) async-start(bf16[32,2,128,128]{3,2,1,0:T(8,128)(2,1)} %stack.2), calls=%async_computation | async-start | bytes 4194304 | tf_op jit(solution)/shard_map/all_to_all | solution.py:50
  26.2 0.0 reduce-scatter.7.cloned.1.call-start
  26.3 1.3 copy.32
  27.5 1.5 copy.33
  29.1 0.1 iota_compare_fusion
  29.2 0.1 lt.72
  29.3 0.0 copy-start.7
  29.3 3.1 gather_fusion.1
  32.4 86.3 %all-to-all-done = bf16[32,2,128,128]{3,2,1,0:T(8,128)(2,1)S(1)} async-done(((bf16[32,2,128,128]{3,2,1,0:T(8,128)(2,1)}), bf16[32,2,128,128]{3,2,1,0:T(8,128)(2,1)S(1)}, u32[]{:S(2)}, u32[]{:S(2)}) %all-to-all-start) | async-done | bytes 2097184 | tf_op jit(solution)/shard_map/all_to_all | solution.py:50
  118.8 0.4 bitcast_select_fusion
  119.1 2.6 copy-done.2
  121.7 4.5 fusion.2
  126.2 2.4 broadcast_in_dim.57
  128.7 19.4 %scatter_fusion.1 = f32[256,32,128]{2,0,1:T(8,128)} fusion(f32[256,32,128]{2,0,1:T(8,128)} %broadcast_in_dim.57, s32[64]{0:T(128)S(1)} %fusion.18, f32[64,256,128]{2,1,0:T(8,128)} %fusion.2), kind=kCustom, calls=%fused_computation.3 | custom fusion | flops 2097152 | bytes 25166080 | tf_op jit(solution)/shard_map/scatter-add | solution.py:28
  148.0 2.5 convert_element_type.28
  150.6 2.9 copy.34
  153.5 4.1 copy.39
  157.6 0.0 reduce-scatter.7.cloned.1.call-update
  157.7 0.0 all-gather.2.cloned.1.call-start
  157.7 0.2 fusion.15
  157.9 144.6 %reduce-scatter.7.cloned.1.call-done = bf16[32,4096]{1,0:T(8,128)(2,1)} async-done(((bf16[256,4096]{1,0:T(8,128)(2,1)}), bf16[32,4096]{1,0:T(8,128)(2,1)}) %reduce-scatter.7.cloned.1.call-update) | async-done | bytes 262160 | tf_op jit(solution)/shard_map/reduce_scatter | solution.py:55
  302.5 1.3 fusion.16
  303.8 1.9 fusion.12
  305.7 0.0 all-gather.2.cloned.1.call-update
  305.7 0.0 reduce-scatter.5.cloned.1.call-start
  305.8 110.0 %all-gather.2.cloned.1.call-done = bf16[256,4096]{1,0:T(8,128)(2,1)} async-done(((bf16[32,4096]{1,0:T(8,128)(2,1)}), bf16[256,4096]{1,0:T(8,128)(2,1)}) %all-gather.2.cloned.1.call-update) | async-done | bytes 2097168 | tf_op jit(solution)/shard_map/all_gather | solution.py:47
  415.8 4.1 copy.29
  419.8 3.2 copy.30
  423.1 3.0 gather_fusion
  426.1 7.0 fusion
  433.1 0.0 reduce-scatter.5.cloned.1.call-update
  433.1 0.0 all-reduce.2.cloned.1.call-start
  433.2 0.6 constant_dynamic-slice_fusion
  433.8 0.6 iota_compare_fusion.1
  434.4 103.1 %psum.14 = f32[4096]{0:T(1024)} all-reduce(f32[4096]{0:T(1024)S(1)} %get-tuple-element.18), channel_id=1, replica_groups=mesh['dp'=2,'fsdp'=32,'tensor'=8] {'dp','fsdp','tensor'}, use_global_device_ids=true, to_apply=%region_6.9 | all-reduce | flops 4096 | bytes 32768 | tf_op jit(solution)/shard_map/psum | solution.py:74
  537.5 121.2 %reduce-scatter.5.cloned.1.call-done = f32[2,128,128]{2,1,0:T(8,128)} async-done(((f32[64,128,128]{2,1,0:T(8,128)}), f32[2,128,128]{2,1,0:T(8,128)}) %reduce-scatter.5.cloned.1.call-update) | async-done | bytes 131088 | tf_op jit(solution)/shard_map/reduce_scatter | solution.py:65
  658.7 1.6 broadcast_select_fusion.6
  660.4 0.0 all-reduce.2.cloned.1.call-update
  660.4 6.7 fusion.5
  667.1 0.2 broadcast_in_dim.54
  667.3 12.4 %scatter_fusion = f32[256,14,128]{2,0,1:T(8,128)S(1)} fusion(f32[256,14,128]{2,0,1:T(8,128)S(1)} %broadcast_in_dim.54, s32[64]{0:T(128)S(1)} %fusion.17, f32[64,256,128]{2,1,0:T(8,128)} %fusion.5), kind=kCustom, calls=%fused_computation.2 | custom fusion | flops 2097152 | bytes 25166080 | tf_op jit(solution)/shard_map/scatter-add | solution.py:15
  679.7 0.2 convert_element_type.26
  679.9 0.5 copy.31
  680.4 1.4 copy.37
  681.8 36.2 %all-reduce.2.cloned.1.call-done = f32[2,128,128]{2,1,0:T(8,128)} async-done(((f32[2,128,128]{2,1,0:T(8,128)}), f32[2,128,128]{2,1,0:T(8,128)}) %all-reduce.2.cloned.1.call-update) | async-done | bytes 131088 | tf_op jit(solution)/shard_map/psum | solution.py:72
  718.0 1.6 copy.44
  (24 shorter events, 0.1 us)
Async XLA Ops:
  7.2 19.1 %copy-start.4 = (bf16[256,1792]{1,0:T(8,128)(2,1)S(1)}, bf16[256,1792]{1,0:T(8,128)(2,1)}, u32[]{:S(2)}) copy-start(bf16[256,1792]{1,0:T(8,128)(2,1)} %param.17) | copy-start | bytes 2752516
  10.0 19.1 %copy-start.6 = (s32[1,32]{1,0:T(1,128)S(1)}, s32[1,32]{1,0:T(1,128)}, u32[]{:S(2)}) copy-start(s32[1,32]{1,0:T(1,128)} %param.16) | copy-start | bytes 388
  10.0 19.3 %copy-start.8 = (s32[1,64]{1,0:T(1,128)S(1)}, s32[1,64]{1,0:T(1,128)}, u32[]{:S(2)}) copy-start(s32[1,64]{1,0:T(1,128)} %param.15) | copy-start | bytes 772
  10.0 108.8 %all-to-all-start = ((bf16[32,2,128,128]{3,2,1,0:T(8,128)(2,1)}), bf16[32,2,128,128]{3,2,1,0:T(8,128)(2,1)S(1)}, u32[]{:S(2)}, u32[]{:S(2)}) async-start(bf16[32,2,128,128]{3,2,1,0:T(8,128)(2,1)} %stack.2), calls=%async_computation | async-start | bytes 4194304 | tf_op jit(solution)/shard_map/all_to_all | solution.py:50
  26.2 276.3 %reduce-scatter.7.cloned.1.call-start = ((), (), s32[]{:S(2)}) async-start(), calls=%async_computation.6 | async-start | bytes 2359296 | tf_op jit(solution)/shard_map/reduce_scatter | solution.py:55
  29.3 3.1 copy-start.7
  118.8 2.9 copy-start.2
  119.1 7.1 copy-start
  153.5 4.2 copy-start.3
  153.5 149.0 %copy-start.5 = (f32[4096]{0:T(1024)S(1)}, f32[4096]{0:T(1024)}, u32[]{:S(2)}) copy-start(f32[4096]{0:T(1024)} %param.12) | copy-start | bytes 49156
  157.7 258.1 %all-gather.2.cloned.1.call-start = ((), (), s32[]{:S(2)}) async-start(), calls=%async_computation.3 | async-start | bytes 2359296 | tf_op jit(solution)/shard_map/all_gather | solution.py:47
  305.7 353.0 %reduce-scatter.5.cloned.1.call-start = ((), (), s32[]{:S(2)}) async-start(), calls=%async_computation.4 | async-start | bytes 4325376 | tf_op jit(solution)/shard_map/reduce_scatter | solution.py:65
  433.1 227.3 %copy-start.1 = (bf16[64,128,128]{2,1,0:T(8,128)(2,1)S(1)}, bf16[64,128,128]{2,1,0:T(8,128)(2,1)}, u32[]{:S(2)}) copy-start(bf16[64,128,128]{2,1,0:T(8,128)(2,1)} %copy-done) | copy-start | bytes 6291460
  433.1 284.8 %all-reduce.2.cloned.1.call-start = ((), (), s32[]{:S(2)}) async-start(), calls=%async_computation.5 | async-start | bytes 262144 | tf_op jit(solution)/shard_map/psum | solution.py:72
Sparse Core Ops, SparseCore 0:
  157.8 144.6 reduce-scatter.6
  306.7 108.9 all-gather.1
  433.2 225.4 reduce-scatter.4
  662.3 55.6 all-reduce.1
